TPU v7x, 256 devices: a whole 4x4x8 slice. The times are simulated.
256 devices in a mesh: frame: 16 (over x_lo, y, core), head: 16 (over z, x_hi).
Axes of the slice: x: 4 (x_hi: 2, x_lo: 2; x = x_hi * 2 + x_lo), y: 4, z: 8, core: 2. Of those that a mesh axis runs over, the one named last changes fastest.
Arguments:
- video: bfloat16 [32768, 1536], P(('frame', 'head')), may hold values from -6 to 6
- audio_keys: bfloat16 [32768, 1536], P(('frame', 'head')), may hold values from -240 to 240
- audio_values: bfloat16 [32768, 1536], P(('frame', 'head')), may hold values from -6 to 6
- query_weight: bfloat16 [1536, 1536], P(('frame', 'head')), may hold values from -0.15625 to 0.15625
- d_out: bfloat16 [32768, 1536], P(('frame', 'head')), may hold values from -6 to 6
- win_start: int32 [256], P(('frame', 'head')), may hold values from 0 to 255
- win_count: int32 [256], P(('frame', 'head')), may hold values from 1 to 5, as said below
Outputs:
- attended: bfloat16 [32768, 1536], P(('frame', 'head'))
- grad_video: bfloat16 [32768, 1536], P(('frame', 'head'))
- grad_query_weight: float32 [1536, 1536], P(('frame', 'head'))
- grad_keys: float32 [32768, 1536], P(('frame', 'head'))
- grad_values: float32 [32768, 1536], P(('frame', 'head'))
Inputs may be any that keep to these rules, and one draw needn't show every extreme that they name: `win_count`: each frame group's window lies within 2 blocks of the block with the same index as the group's device (group g on device g) and within the 256 blocks; some group has a window of 5 blocks.
All inputs are finite; a program needn't handle non-finite values.
Results may differ from a plain program's by a relative error of at most 0.04.
The roundings to bfloat16 on the way count: a program that leaves them out, or rounds other values in their place, can miss the bound.
Values may be sent and summed in bfloat16 or wider, within the bound.
A program may use at most 128 MiB of HBM per device.

v0:
```python
import math

import jax
import jax.numpy as jnp
from jax import lax
from jax.sharding import PartitionSpec as P

HEADS = 12
HEAD_DIM = 128
GROUP = 128
REACH = 2


def from_behind(block, axis, distance):
    devices = range(lax.axis_size(axis))
    route = [(i - distance, i) for i in devices if i - distance in devices]
    return lax.ppermute(block, axis, route)


def attend(queries, key_rows, value_rows, grad_rows, allowed):
    row_count = queries.shape[0]
    length = key_rows.shape[0]
    head_count = queries.shape[1] // HEAD_DIM
    scaling = 1.0 / math.sqrt(HEAD_DIM)
    query_heads = queries.reshape(row_count, head_count, HEAD_DIM)
    key_heads = key_rows.reshape(length, head_count, HEAD_DIM)
    value_heads = value_rows.reshape(length, head_count, HEAD_DIM)
    grad_heads = grad_rows.reshape(row_count, head_count, HEAD_DIM)
    scores = (
        jnp.einsum("rhd,lhd->hrl", query_heads, key_heads, preferred_element_type=jnp.float32)
        * scaling
    )
    scores = jnp.where(allowed[None], scores, -1e30)
    top_score = jnp.max(scores, axis=-1, keepdims=True)
    exponent = jnp.exp(scores - top_score)
    probs_full = exponent / jnp.sum(exponent, axis=-1, keepdims=True)
    probs_half = probs_full.astype(jnp.bfloat16)
    attended = jnp.einsum(
        "hrl,lhd->rhd", probs_half, value_heads, preferred_element_type=jnp.float32
    )
    attended = attended.astype(jnp.bfloat16).reshape(row_count, head_count * HEAD_DIM)
    prob_grad = jnp.einsum(
        "rhd,lhd->hrl", grad_heads, value_heads, preferred_element_type=jnp.float32
    )
    row_delta = jnp.sum(probs_full * prob_grad, axis=-1, keepdims=True)
    score_grad = (probs_full * (prob_grad - row_delta) * scaling).astype(jnp.bfloat16)
    query_grad = jnp.einsum(
        "hrl,lhd->rhd", score_grad, key_heads, preferred_element_type=jnp.float32
    )
    query_grad = query_grad.astype(jnp.bfloat16).reshape(row_count, head_count * HEAD_DIM)
    key_grad = jnp.einsum(
        "hrl,rhd->lhd", score_grad, query_heads, preferred_element_type=jnp.float32
    )
    value_grad = jnp.einsum(
        "hrl,rhd->lhd", probs_half, grad_heads, preferred_element_type=jnp.float32
    )
    return (
        attended,
        query_grad,
        key_grad.reshape(length, head_count * HEAD_DIM),
        value_grad.reshape(length, head_count * HEAD_DIM),
    )


def attend_groups(queries, key_rows, value_rows, grad_rows, allowed):
    per_group = math.gcd(HEADS, 4)
    width = per_group * HEAD_DIM
    results = []
    for first in range(0, HEADS, per_group):
        begin = first * HEAD_DIM
        results.append(
            attend(
                queries[:, begin : begin + width],
                key_rows[:, begin : begin + width],
                value_rows[:, begin : begin + width],
                grad_rows[:, begin : begin + width],
                allowed,
            )
        )
    return tuple((jnp.concatenate([item[k] for item in results], axis=1) for k in range(4)))


def shards(video, audio_keys, audio_values, query_weight, d_out, win_start, win_count):
    position = lax.axis_index(("frame", "head"))
    audio_rows = audio_keys.shape[0]
    row_count = video.shape[0]
    weight_full = lax.all_gather(query_weight, ("frame", "head"), axis=0, tiled=True)
    queries = jnp.dot(video, weight_full, preferred_element_type=jnp.float32).astype(jnp.bfloat16)
    stacked = jnp.stack([audio_keys, audio_values])
    pieces = {0: stacked}
    for offset in range(-REACH, REACH + 1):
        if offset != 0:
            pieces[offset] = from_behind(stacked, ("frame", "head"), -offset)
    window = jnp.concatenate([pieces[offset] for offset in range(-REACH, REACH + 1)], axis=1)
    length = window.shape[1]
    row_start = jnp.repeat(win_start, GROUP, total_repeat_length=row_count)
    row_end = row_start + jnp.repeat(win_count, GROUP, total_repeat_length=row_count)
    key_block = position - REACH + jnp.arange(length, dtype=jnp.int32) // audio_rows
    allowed = (key_block[None, :] >= row_start[:, None]) & (key_block[None, :] < row_end[:, None])
    attended, query_grad, key_grad, value_grad = attend_groups(
        queries, window[0], window[1], d_out, allowed
    )
    contrib = jnp.stack([key_grad, value_grad])
    parts = {}
    for offset in range(-REACH, REACH + 1):
        begin = (offset + REACH) * audio_rows
        parts[offset] = contrib[:, begin : begin + audio_rows]
    total = parts[0]
    for offset in range(-REACH, REACH + 1):
        if offset != 0:
            total = total + from_behind(
                parts[offset].astype(jnp.bfloat16), ("frame", "head"), offset
            ).astype(jnp.float32)
    grad_video = jnp.einsum(
        "rj,ij->ri", query_grad, weight_full, preferred_element_type=jnp.float32
    ).astype(jnp.bfloat16)
    weight_term = jnp.einsum("ri,rj->ij", video, query_grad, preferred_element_type=jnp.float32)
    weight_grad = lax.psum_scatter(weight_term, ("frame", "head"), scatter_dimension=0, tiled=True)
    return (attended, grad_video, weight_grad, total[0], total[1])


def solution(mesh):
    return jax.shard_map(
        shards,
        mesh=mesh,
        in_specs=(
            P(("frame", "head"), None),
            P(("frame", "head"), None),
            P(("frame", "head"), None),
            P(("frame", "head"), None),
            P(("frame", "head"), None),
            P(("frame", "head")),
            P(("frame", "head")),
        ),
        out_specs=(
            P(("frame", "head"), None),
            P(("frame", "head"), None),
            P(("frame", "head"), None),
            P(("frame", "head"), None),
            P(("frame", "head"), None),
        ),
        check_vma=False,
    )
```

profile of v0, /device:TPU:32, one launch (start us, length us, event | category | flops | bytes accessed | tf_op | source)
XLA Modules:
  0.0 1120.2 jit_solution(14979720353040239099)
XLA Ops:
  8.0 1.2 copy.76
  9.2 1.2 copy.77
  10.5 3.8 collective-permute-start
  14.3 4.9 collective-permute-start.1
  19.3 3.7 collective-permute-start.3
  23.0 1.9 collective-permute-start.2
  26.3 1.8 fusion.111
  28.0 1.7 copy.123
  29.7 1.7 copy.124
  31.4 1.7 copy.125
  33.0 1.3 constant_dynamic-update-slice_fusion.4
  34.3 16.9 %collective-permute-done.1 = bf16[2,128,1536]{1,2,0:T(8,128)(2,1)} collective-permute-done((bf16[2,128,1536]{1,2,0:T(8,128)(2,1)S(1)}, bf16[2,128,1536]{1,2,0:T(8,128)(2,1)}, u32[]{:S(2)}, u32[]{:S(2)}) %collective-permute-start.1) | collective-permute-done | bytes 786464 | tf_op jit(solution)/shard_map/ppermute | solution.py:17
  51.2 1.3 constant_dynamic-update-slice_fusion.3
  52.7 8.2 collective-permute-done.2
  61.7 1.4 fusion.109
  63.1 1.4 convolution_bitcast_fusion.2
  65.5 1.4 convolution_bitcast_fusion.3
  66.9 671.8 %all-gather.3.cloned.1.call-done = bf16[256,6,1536]{2,1,0:T(8,128)(2,1)} async-done(((bf16[1,6,1536]{2,1,0:T(8,128)(2,1)}), bf16[256,6,1536]{2,1,0:T(8,128)(2,1)}) %all-gather.3.cloned.1.call-update) | async-done | bytes 4718608 | tf_op jit(solution)/shard_map/all_gather | solution.py:87
  738.7 8.4 reshape.266
  747.1 3.1 convolution_convert_fusion.1
  750.9 0.8 copy.128
  751.7 2.8 fusion.113
  754.5 2.6 convolution_convert_fusion.2
  757.1 4.5 fusion.60
  761.6 5.3 fusion.35
  766.9 2.9 fusion.69
  769.8 1.7 copy.126
  771.6 2.8 fusion.115
  774.4 1.7 fusion.114
  776.1 5.4 fusion.54
  781.6 5.1 fusion.57
  786.7 5.0 convolution_bitcast_fusion
  791.8 1.1 copy-done.11
  792.9 0.8 convolution_convert_fusion.4
  794.3 1.7 copy.107
  796.0 0.8 copy.84
  796.8 6.3 fusion.49
  803.0 2.8 copy.102
  805.9 3.3 fusion.75
  809.1 2.8 copy.105
  811.9 6.3 fusion.42
  818.2 2.8 copy.103
  821.0 3.1 fusion.72
  824.1 2.9 copy.106
  827.0 2.2 maximum_bitcast_fusion
  829.8 1.7 copy-done.2
  832.2 1.3 copy-done.4
  833.5 1.5 fusion.108
  835.0 2.4 collective-permute-start.4
  837.3 5.3 collective-permute-start.7
  842.7 1.9 collective-permute-start.6
  844.6 6.5 collective-permute-start.5
  851.1 2.7 convolution_convert_fusion.3
  853.8 1.0 copy.85
  854.8 1.7 pad_maximum_fusion.2
  856.5 4.9 convolution_convert_fusion
  861.4 5.9 collective-permute-done.4
  867.3 17.2 %collective-permute-done.6 = bf16[2,128,1536]{2,1,0:T(8,128)(2,1)} collective-permute-done((bf16[2,128,1536]{2,1,0:T(8,128)(2,1)}, bf16[2,128,1536]{2,1,0:T(8,128)(2,1)}, u32[]{:S(2)}, u32[]{:S(2)}) %collective-permute-start.6) | collective-permute-done | bytes 786464 | tf_op jit(solution)/shard_map/ppermute | solution.py:17
  884.5 4.2 collective-permute-done.5
  888.7 2.1 fusion.14
  890.8 1.2 slice_bitcast_fusion.2
  892.1 218.7 %all-reduce.3.cloned.1.call-done = f32[1536,1536]{0,1:T(8,128)} async-done(((f32[1536,1536]{0,1:T(8,128)}), f32[1536,1536]{0,1:T(8,128)}) %all-reduce.3.cloned.1.call-update) | async-done | bytes 9437200
  1110.8 1.7 constant_dynamic-slice_fusion
  1112.5 0.9 copy.108
  (69 shorter events, 5.4 us)
Async XLA Ops:
  7.2 740.0 %copy-start = (bf16[128,1536]{1,0:T(8,128)(2,1)S(1)}, bf16[128,1536]{1,0:T(8,128)(2,1)}, u32[]{:S(2)}) copy-start(bf16[128,1536]{1,0:T(8,128)(2,1)} %param.17) | copy-start | bytes 1179652
  7.2 731.6 %all-gather.3.cloned.1.call-start = ((), (), s32[]{:S(2)}) async-start(), calls=%async_computation | async-start | bytes 6316032 | tf_op jit(solution)/shard_map/all_gather | solution.py:87
  7.9 1102.9 %all-reduce.3.cloned.1.call-start = ((), (), s32[]{:S(2)}) async-start(), calls=%async_computation.1 | async-start | bytes 18874368
  10.5 22.5 %collective-permute-start = (bf16[2,128,1536]{1,2,0:T(8,128)(2,1)S(1)}, bf16[2,128,1536]{1,2,0:T(8,128)(2,1)}, u32[]{:S(2)}, u32[]{:S(2)}) collective-permute-start(bf16[2,128,1536]{1,2,0:T(8,128)(2,1)S(1)} %pad_maximum_fusion.1), channel_id=1, source_target_pairs={{0,2},{1,3},{2,4},{3,5},{4,6},{5,7},{6,8},{7,9},{8,10},{9,11},{10,... | collective-permute-start | bytes 2359304 | tf_op jit(solution)/shard_map/ppermute | solution.py:17
  14.3 36.9 %collective-permute-start.1 = (bf16[2,128,1536]{1,2,0:T(8,128)(2,1)S(1)}, bf16[2,128,1536]{1,2,0:T(8,128)(2,1)}, u32[]{:S(2)}, u32[]{:S(2)}) collective-permute-start(bf16[2,128,1536]{1,2,0:T(8,128)(2,1)S(1)} %pad_maximum_fusion.1), channel_id=1, source_target_pairs={{0,1},{1,2},{2,3},{3,4},{4,5},{5,6},{6,7},{7,8},{8,9},{9,10},{10,1... | collective-permute-start | bytes 2359304 | tf_op jit(solution)/shard_map/ppermute | solution.py:17
  19.3 41.9 %collective-permute-start.3 = (bf16[2,128,1536]{1,2,0:T(8,128)(2,1)S(1)}, bf16[2,128,1536]{1,2,0:T(8,128)(2,1)S(1)}, u32[]{:S(2)}, u32[]{:S(2)}) collective-permute-start(bf16[2,128,1536]{1,2,0:T(8,128)(2,1)S(1)} %pad_maximum_fusion.1), channel_id=1, source_target_pairs={{2,0},{3,1},{4,2},{5,3},{6,4},{7,5},{8,6},{9,7},{10,8},{11,9},{12,... | collective-permute-start | bytes 2359304 | tf_op jit(solution)/shard_map/ppermute | solution.py:17
  23.0 37.9 %collective-permute-start.2 = (bf16[2,128,1536]{1,2,0:T(8,128)(2,1)S(1)}, bf16[2,128,1536]{1,2,0:T(8,128)(2,1)S(1)}, u32[]{:S(2)}, u32[]{:S(2)}) collective-permute-start(bf16[2,128,1536]{1,2,0:T(8,128)(2,1)S(1)} %pad_maximum_fusion.1), channel_id=1, source_target_pairs={{1,0},{2,1},{3,2},{4,3},{5,4},{6,5},{7,6},{8,7},{9,8},{10,9},{11,1... | collective-permute-start | bytes 2359304 | tf_op jit(solution)/shard_map/ppermute | solution.py:17
  61.7 1.4 copy-start.17
  63.1 1.8 copy-start.7
  63.1 1.5 copy-start.20
  64.5 0.9 copy-start.18
  64.9 692.2 %copy-start.9 = (f32[4,128,640]{2,1,0:T(8,128)}, f32[4,128,640]{2,1,0:T(8,128)S(1)}, u32[]{:S(2)}) copy-start(f32[4,128,640]{2,1,0:T(8,128)S(1)} %convolution_bitcast_fusion.1) | copy-start | bytes 3932164
  751.7 2.8 copy-start.25
  761.6 5.3 copy-start.12
  771.6 4.6 copy-start.21
  771.6 2.8 copy-start.10
  781.6 5.2 copy-start.13
  786.7 5.0 copy-start.15
  791.8 1.1 copy-start.11
  791.8 1.1 copy-start.23
  792.9 0.9 copy-start.24
  803.0 2.8 copy-start.19
  809.1 2.8 copy-start.22
  827.0 2.2 copy-start.5
  827.0 2.6 copy-start.6
  829.5 2.0 copy-start.2
  831.5 2.0 copy-start.4
  833.5 17.6 %copy-start.8 = (bf16[640,512]{0,1:T(8,128)(2,1)S(1)}, bf16[640,512]{0,1:T(8,128)(2,1)}, u32[]{:S(2)}) copy-start(bf16[640,512]{0,1:T(8,128)(2,1)} %copy-done.7) | copy-start | bytes 1966084
  835.0 32.3 %collective-permute-start.4 = (bf16[2,128,1536]{2,1,0:T(8,128)(2,1)}, bf16[2,128,1536]{2,1,0:T(8,128)(2,1)S(1)}, u32[]{:S(2)}, u32[]{:S(2)}) collective-permute-start(bf16[2,128,1536]{2,1,0:T(8,128)(2,1)} %get-tuple-element.61), channel_id=1, source_target_pairs={{2,0},{3,1},{4,2},{5,3},{6,4},{7,5},{8,6},{9,7},{10,8},{11,9},{12,... | collective-permute-start | bytes 2359304 | tf_op jit(solution)/shard_map/ppermute | solution.py:17
  837.3 30.0 %collective-permute-start.7 = (bf16[2,128,1536]{2,1,0:T(8,128)(2,1)}, bf16[2,128,1536]{2,1,0:T(8,128)(2,1)S(1)}, u32[]{:S(2)}, u32[]{:S(2)}) collective-permute-start(bf16[2,128,1536]{2,1,0:T(8,128)(2,1)} %get-tuple-element.62), channel_id=1, source_target_pairs={{0,2},{1,3},{2,4},{3,5},{4,6},{5,7},{6,8},{7,9},{8,10},{9,11},{10,... | collective-permute-start | bytes 2359304 | tf_op jit(solution)/shard_map/ppermute | solution.py:17
  842.7 41.8 %collective-permute-start.6 = (bf16[2,128,1536]{2,1,0:T(8,128)(2,1)}, bf16[2,128,1536]{2,1,0:T(8,128)(2,1)}, u32[]{:S(2)}, u32[]{:S(2)}) collective-permute-start(bf16[2,128,1536]{2,1,0:T(8,128)(2,1)} %get-tuple-element.63), channel_id=1, source_target_pairs={{0,1},{1,2},{2,3},{3,4},{4,5},{5,6},{6,7},{7,8},{8,9},{9,10},{10,1... | collective-permute-start | bytes 2359304 | tf_op jit(solution)/shard_map/ppermute | solution.py:17
  844.6 11.9 %copy-start.14 = (bf16[4,128,128]{2,1,0:T(8,128)(2,1)S(1)}, bf16[4,128,128]{2,1,0:T(8,128)(2,1)}, u32[]{:S(2)}) copy-start(bf16[4,128,128]{2,1,0:T(8,128)(2,1)} %copy-done.13) | copy-start | bytes 393220
  844.6 11.9 %copy-start.16 = (bf16[4,128,128]{2,1,0:T(8,128)(2,1)S(1)}, bf16[4,128,128]{2,1,0:T(8,128)(2,1)}, u32[]{:S(2)}) copy-start(bf16[4,128,128]{2,1,0:T(8,128)(2,1)} %copy-done.15) | copy-start | bytes 393220
  844.6 44.0 %collective-permute-start.5 = (bf16[2,128,1536]{2,1,0:T(8,128)(2,1)S(1)}, bf16[2,128,1536]{2,1,0:T(8,128)(2,1)}, u32[]{:S(2)}, u32[]{:S(2)}) collective-permute-start(bf16[2,128,1536]{2,1,0:T(8,128)(2,1)S(1)} %get-tuple-element.64), channel_id=1, source_target_pairs={{1,0},{2,1},{3,2},{4,3},{5,4},{6,5},{7,6},{8,7},{9,8},{10,9},{11,1... | collective-permute-start | bytes 2359304 | tf_op jit(solution)/shard_map/ppermute | solution.py:17
  856.5 32.2 %copy-start.3 = (f32[1,640,1536]{2,1,0:T(8,128)S(1)}, f32[1,640,1536]{2,1,0:T(8,128)}, u32[]{:S(2)}) copy-start(f32[1,640,1536]{2,1,0:T(8,128)} %copy-done.2) | copy-start | bytes 11796484
  890.8 222.6 %copy-start.1 = (bf16[128,1536]{1,0:T(8,128)(2,1)S(1)}, bf16[128,1536]{1,0:T(8,128)(2,1)}, u32[]{:S(2)}) copy-start(bf16[128,1536]{1,0:T(8,128)(2,1)} %param.17) | copy-start | bytes 1179652
Sparse Core Ops, SparseCore 0:
  9.9 728.7 all-gather.2
  791.9 318.8 all-reduce.2
where the time goes:
time: 1120 us
  waiting for transfers between devices  944 us (84%)
  matrix products  71.8 us (6%)
  local copies, waits for them, and re-layouts  51.2 us (5%)
  starting transfers between devices  30.6 us (3%)
  between operations  15.7 us (1%)
    all_gather x1, waiting for transfers between devices, shards(): lax.all_gather(query_weight, ('frame', 'head'), axis=0, tiled=True)  672 us
    unnamed x3, waiting for transfers between devices  219 us
    ppermute x8, waiting for transfers between devices, from_behind(): return lax.ppermute(block, axis, route)  52.3 us
    ppermute x8, starting transfers between devices, from_behind(): return lax.ppermute(block, axis, route)  30.5 us
    unnamed x63, local copies, waits for them, and re-layouts  26.2 us
  transfers between devices with their start and end apart: 10, of which 7 were waited for; matrix products, arithmetic and copies ran while one was open for 6% of the time, Pallas kernels for 0%

commit v1 on v0

v1 whole, which is shorter than its diff:
```python
import math

import jax
import jax.numpy as jnp
from jax import lax
from jax.experimental import pallas as pl
from jax.experimental.pallas import tpu as pltpu
from jax.sharding import PartitionSpec as P

MESH = pl.DeviceIdType.MESH
HD = 128
D = 1536
HALF = 768
ROWS = 128
NG = 3
GW = HALF // NG
FR = 96
SCALE = 1.0 / math.sqrt(HD)
F32 = jnp.float32
BF16 = jnp.bfloat16
NSEM = 128


def dot(a, b, ca, cb):
    return lax.dot_general(a, b, (((ca,), (cb,)), ((), ())), preferred_element_type=F32)


def kernel(
    ws_ref, wc_ref, video, keys, values, d_out, w_ref,
    att_out, gvid_out, wg_out, gk_out, gv_out,
    ssem, rsem, lsem,
    win, wf, w_send, w_small, w_full, w_tmp,
    vid, vid_t, k_buf, v_buf, do_buf, q_buf, mask, att_buf, qg_buf,
    gh_send, gh_recv, g_mid, x_send, x_recv, gv_send, gv_recv, gv_own,
    wgp, e_recv, d_own, d_send, d_recv, c_part, c_recv, b_tmp, b_part, b_recv, a_part, a_recv,
):
    f = lax.axis_index("frame")
    h = lax.axis_index("head")
    s = lax.rem(h, 2)
    z = h // 2
    x_lo = f // 8
    y = lax.rem(f // 2, 4)
    core = lax.rem(f, 2)
    p = f * 16 + h

    partner = (f, z * 2 + 1 - s)

    def z_dev(d):
        return (f, lax.rem(z + d, 8) * 2 + s)

    def y_of(d):
        return lax.rem(y + d, 4)

    def y_dev(d):
        return (x_lo * 8 + y_of(d) * 2 + core, h)

    xlo_dev = ((1 - x_lo) * 8 + y * 2 + core, h)
    core_dev = (x_lo * 8 + y * 2 + 1 - core, h)

    def halo_dev(d):
        q = lax.rem(p + d + 256, 256)
        return (q // 16, lax.rem(q, 16))

    def mine(g):
        return pl.ds(pl.multiple_of(s * HALF + g * GW, 128), GW)

    def theirs(g):
        return pl.ds(pl.multiple_of((1 - s) * HALF + g * GW, 128), GW)

    count = [0]
    sent = []

    def remote(src, dst, dev):
        i = count[0]
        count[0] += 1
        cp = pltpu.make_async_remote_copy(
            src_ref=src, dst_ref=dst, send_sem=ssem.at[i], recv_sem=rsem.at[i],
            device_id=dev, device_id_type=MESH,
        )
        sent.append(cp)
        return cp

    local = [
        pltpu.make_async_copy(video, vid.at[0:ROWS], lsem.at[0]),
        pltpu.make_async_copy(keys.at[:, pl.ds(pl.multiple_of(s * HALF, 128), HALF)], k_buf.at[256:384], lsem.at[1]),
        pltpu.make_async_copy(values.at[:, pl.ds(pl.multiple_of(s * HALF, 128), HALF)], v_buf.at[256:384], lsem.at[2]),
        pltpu.make_async_copy(d_out.at[:, pl.ds(pl.multiple_of(s * HALF, 128), HALF)], do_buf.at[0:ROWS], lsem.at[3]),
    ]
    for cp in local:
        cp.start()

    barrier = pltpu.get_barrier_semaphore()
    peers = [partner] + [z_dev(d) for d in range(1, 8)] + [y_dev(d) for d in range(1, 4)]
    peers += [xlo_dev, core_dev, halo_dev(-2), halo_dev(2)]
    for dev in peers:
        pl.semaphore_signal(barrier, inc=1, device_id=dev, device_id_type=MESH)

    win[0, 0] = jnp.full((8, 128), ws_ref[0], jnp.int32)
    win[0, 1] = jnp.full((8, 128), ws_ref[0] + wc_ref[0], jnp.int32)
    wf[...] = jnp.zeros_like(wf)
    wf[0:6, :] = w_ref[...].astype(F32)
    for k in range(2):
        for ct in range(0, 6, 2):
            col = k * HALF + ct * 128
            pair = jnp.concatenate([wf[:, col : col + 128], wf[:, col + 128 : col + 256]], axis=0)
            w_send[k, ct * 8 : ct * 8 + 16, :] = pair.astype(BF16)

    pl.semaphore_wait(barrier, len(peers))

    wa = remote(w_send.at[1 - s], w_small.at[h], partner)
    wa.start()
    wl = pltpu.make_async_copy(w_send.at[s], w_small.at[h], lsem.at[4])
    wl.start()
    win_cp = remote(win.at[0], win.at[1], partner)
    win_cp.start()
    kx, vx, dx = [], [], []
    for g in range(NG):
        c = pl.ds(g * GW, GW)
        kx.append(remote(keys.at[:, theirs(g)], k_buf.at[384:512, c], partner))
        vx.append(remote(values.at[:, theirs(g)], v_buf.at[384:512, c], partner))
        kx[g].start()
        vx[g].start()
    vid_cp = remote(video, vid.at[ROWS : 2 * ROWS], partner)
    vid_cp.start()
    for g in range(NG):
        c = pl.ds(g * GW, GW)
        dx.append(remote(d_out.at[:, theirs(g)], do_buf.at[ROWS : 2 * ROWS, c], partner))
        dx[g].start()

    wl.wait()
    wa.wait_recv()
    zb = []
    for d in range(1, 8):
        pair = w_small.at[pl.ds(z * 2, 2)]
        zb.append(remote(pair, pair, z_dev(d)))
        zb[-1].start()

    halo_own = []
    for g in range(NG):
        c = pl.ds(g * GW, GW)
        for d in (-2, 2):
            at = 0 if d == 2 else 512
            halo_own.append(remote(keys.at[:, mine(g)], k_buf.at[at : at + 128, c], halo_dev(d)))
            halo_own.append(remote(values.at[:, mine(g)], v_buf.at[at : at + 128, c], halo_dev(d)))
    for cp in halo_own:
        cp.start()

    for cp in zb:
        cp.wait_recv()
    for i in range(16):
        rows = w_small[i].astype(F32)
        for ct in range(6):
            w_tmp[6 * i : 6 * i + 8, ct * 128 : ct * 128 + 128] = rows[ct * 8 : ct * 8 + 8, :]
    me = pl.ds(pl.multiple_of(f * FR, FR), FR)
    w_full[me, :] = w_tmp[0:FR, :].astype(BF16)

    def frame_rows(xl, yy, cc):
        return w_full.at[pl.ds(pl.multiple_of((xl * 8 + yy * 2 + cc) * FR, FR), FR)]

    chunk = frame_rows(x_lo, y, core)
    cx = remote(chunk, chunk, xlo_dev)
    cx.start()
    dy, e_cps = [], []
    for d in range(1, 4):
        dy.append(remote(chunk, chunk, y_dev(d)))
        dy[-1].start()
    e_cps.append(remote(chunk, chunk, core_dev))
    e_cps[-1].start()

    halo_par = []

    def pass_on(g):
        c = pl.ds(g * GW, GW)
        kx[g].wait_recv()
        vx[g].wait_recv()
        for d in (-2, 2):
            at = 128 if d == 2 else 640
            for buf in (k_buf, v_buf):
                halo_par.append(remote(buf.at[384:512, c], buf.at[at : at + 128, c], halo_dev(d)))
                halo_par[-1].start()

    pass_on(0)
    cx.wait_recv()
    chunk2 = frame_rows(1 - x_lo, y, core)
    for d in range(1, 4):
        dy.append(remote(chunk2, chunk2, y_dev(d)))
        dy[-1].start()
    e_cps.append(remote(chunk2, chunk2, core_dev))
    e_cps[-1].start()
    pass_on(1)
    pass_on(2)

    win_cp.wait_recv()
    for half in range(2):
        lo = win[half, 0, 0:1, :]
        hi = win[half, 1, 0:1, :]
        for j in range(6):
            base = p if j % 2 == 0 else p + 1 - 2 * s
            blk = base + 2 * (j // 2 - 1)
            ok = jnp.logical_and(lo <= blk, blk < hi)
            bias = jnp.where(ok, 0.0, -1e30).astype(F32)
            mask[half * 128 : half * 128 + 128, j * 128 : j * 128 + 128] = jnp.broadcast_to(bias, (128, 128))

    for i, cp in enumerate(dy):
        cp.wait_recv()
        d = i % 3 + 1
        got = frame_rows(x_lo if i < 3 else 1 - x_lo, lax.rem(y + 4 - d, 4), core)
        e_cps.append(remote(got, got, core_dev))
        e_cps[-1].start()

    for cp in local:
        cp.wait()
    vid_cp.wait_recv()
    for i in range(0, D, 256):
        vid_t[i : i + 256, :] = vid[:, i : i + 256].T
    for cp in e_cps:
        cp.wait_recv()

    att_cps, gh_cps, xr_cps = [], [], []

    def attention(g):
        c0 = g * GW
        q_buf[:, c0 : c0 + GW] = dot(vid[...], w_full[:, c0 : c0 + GW], 1, 0).astype(BF16)
        for cp in halo_own[4 * g : 4 * g + 4] + halo_par[4 * g : 4 * g + 4]:
            cp.wait_recv()
        dx[g].wait_recv()

        def one(hh, carry):
            c = pl.ds(pl.multiple_of(c0 + hh * HD, 128), HD)
            q = q_buf[:, c]
            k = k_buf[:, c]
            v = v_buf[:, c]
            do = do_buf[:, c]
            sc = dot(q, k, 1, 1) * SCALE + mask[...]
            top = jnp.max(sc, axis=-1, keepdims=True)
            e = jnp.exp(sc - top)
            prob = e * (1.0 / jnp.sum(e, axis=-1, keepdims=True))
            half = prob.astype(BF16)
            att_buf[:, c] = dot(half, v, 1, 0).astype(BF16)
            pg = dot(do, v, 1, 1)
            delta = jnp.sum(prob * pg, axis=-1, keepdims=True)
            ds = (prob * (pg - delta) * SCALE).astype(BF16)
            qg_buf[:, c] = dot(ds, k, 1, 0).astype(BF16)
            gk = dot(ds, q, 0, 0)
            gv = dot(half, do, 0, 0)
            for i, gr in enumerate((gk, gv)):
                gh_send[0, i, :, c] = gr[0:256].astype(BF16)
                g_mid[i, :, c] = gr[256:512]
                gh_send[1, i, :, c] = gr[512:768].astype(BF16)
            return carry

        lax.fori_loop(0, GW // HD, one, 0)
        c = pl.ds(c0, GW)
        for i, d in enumerate((-2, 2)):
            gh_cps.append(remote(gh_send.at[i, :, :, c], gh_recv.at[i, :, :, c], halo_dev(d)))
            gh_cps[-1].start()
        att_cps.append(remote(att_buf.at[ROWS : 2 * ROWS, c], att_out.at[:, mine(g)], partner))
        att_cps[-1].start()
        att_out[:, mine(g)] = att_buf[0:ROWS, c0 : c0 + GW]

    ecs, dcs, ccs, bcs, acs = [], [], [], [], []

    def weight_term(g):
        c0 = g * GW
        for i in range(0, 16, 4):
            r = dot(vid_t[i * FR : (i + 4) * FR, :], qg_buf[:, c0 : c0 + GW], 1, 0)
            for j in range(4):
                fr = i + j
                wgp[g, fr % 2, (fr // 2 % 4) * 2 + fr // 8] = r[j * FR : (j + 1) * FR]
        ecs.append(remote(wgp.at[g, 1 - core], e_recv.at[g], core_dev))
        ecs[g].start()

    def halo_back(g):
        c0 = g * GW
        for cp in gh_cps[2 * g : 2 * g + 2]:
            cp.wait_recv()
        for i, out in enumerate((gk_out, gv_out)):
            tot = g_mid[i, :, c0 : c0 + GW]
            tot = tot + gh_recv[0, i, :, c0 : c0 + GW].astype(F32) + gh_recv[1, i, :, c0 : c0 + GW].astype(F32)
            out[:, mine(g)] = tot[0:ROWS]
            x_send[i, :, c0 : c0 + GW] = tot[ROWS:].astype(BF16)
        c = pl.ds(c0, GW)
        xr_cps.append(remote(x_send.at[:, :, c], x_recv.at[:, :, c], partner))
        xr_cps[-1].start()

    def stage_d(g):
        ecs[g].wait_recv()
        for i in range(8):
            t = wgp[g, core, i] + e_recv[g, i]
            d_own[g, i] = t
            d_send[g, i] = t.astype(BF16)
        cps = []
        for d in range(1, 4):
            cps.append(remote(d_send.at[g, pl.ds(y_of(d) * 2, 2)], d_recv.at[g, d - 1], y_dev(d)))
            cps[-1].start()
        dcs.append(cps)

    def stage_c(g):
        for cp in dcs[g]:
            cp.wait_recv()
        for xl in range(2):
            t = d_own[g, y * 2 + xl]
            for d in range(3):
                t = t + d_recv[g, d, xl].astype(F32)
            c_part[g, xl] = t
        ccs.append(remote(c_part.at[g, 1 - x_lo], c_recv.at[g], xlo_dev))
        ccs[g].start()

    def stage_b(g):
        ccs[g].wait_recv()
        b_tmp[g, 0:FR, :] = c_part[g, x_lo] + c_recv[g]
        for i in range(16):
            b_part[g, i] = b_tmp[g, 6 * i : 6 * i + 8, :]
        cps = []
        for d in range(1, 8):
            cps.append(remote(b_part.at[g, pl.ds(lax.rem(z + d, 8) * 2, 2)], b_recv.at[g, d - 1], z_dev(d)))
            cps[-1].start()
        bcs.append(cps)

    def stage_a(g):
        for cp in bcs[g]:
            cp.wait_recv()
        t = b_part[g, pl.ds(z * 2, 2)]
        for d in range(7):
            t = t + b_recv[g, d]
        a_part[g] = t
        acs.append(remote(a_part.at[g, 1 - s], a_recv.at[g], partner))
        acs[g].start()
        wg_out[:, mine(g)] = a_part[g, s][0:6]

    b_tmp[...] = jnp.zeros_like(b_tmp)
    for g in range(NG):
        attention(g)
        weight_term(g)
        if g > 0:
            halo_back(g - 1)
            stage_d(g - 1)
        if g > 1:
            stage_c(g - 2)

    for i in range(0, D, 512):
        gv_send[:, i : i + 512] = dot(qg_buf[ROWS:, :], w_full[i : i + 512, :], 1, 1).astype(BF16)
    gvc = remote(gv_send, gv_recv, partner)
    gvc.start()
    halo_back(2)
    stage_d(2)
    stage_c(1)
    stage_b(0)
    for i in range(0, D, 512):
        gv_own[:, i : i + 512] = dot(qg_buf[0:ROWS, :], w_full[i : i + 512, :], 1, 1)
    stage_c(2)
    stage_b(1)
    stage_a(0)
    stage_b(2)
    stage_a(1)
    stage_a(2)

    for g in range(NG):
        xr_cps[g].wait_recv()
        c0 = g * GW
        for i, out in enumerate((gk_out, gv_out)):
            out[:, theirs(g)] = x_recv[i, :, c0 : c0 + GW].astype(F32)
    gvc.wait_recv()
    gvid_out[...] = (gv_own[...] + gv_recv[...].astype(F32)).astype(BF16)
    for g in range(NG):
        acs[g].wait_recv()
        wg_out[:, theirs(g)] = a_recv[g][0:6]
        att_cps[g].wait_recv()
    for cp in sent:
        cp.wait_send()
    assert count[0] <= NSEM


def shards(video, audio_keys, audio_values, query_weight, d_out, win_start, win_count):
    V = pltpu.VMEM
    sem = pltpu.SemaphoreType.DMA
    scratch = [
        sem((NSEM,)), sem((NSEM,)), sem((8,)),
        V((2, 2, 8, 128), jnp.int32),
        V((8, D), F32),
        V((2, 48, 128), BF16),
        V((16, 48, 128), BF16),
        V((D, HALF), BF16),
        V((104, HALF), F32),
        V((256, D), BF16),
        V((D, 256), BF16),
        V((768, HALF), BF16),
        V((768, HALF), BF16),
        V((256, HALF), BF16),
        V((256, HALF), BF16),
        V((256, 768), F32),
        V((256, HALF), BF16),
        V((256, HALF), BF16),
        V((2, 2, 256, HALF), BF16),
        V((2, 2, 256, HALF), BF16),
        V((2, 256, HALF), F32),
        V((2, ROWS, HALF), BF16),
        V((2, ROWS, HALF), BF16),
        V((ROWS, D), BF16),
        V((ROWS, D), BF16),
        V((ROWS, D), F32),
        V((NG, 2, 8, FR, GW), F32),
        V((NG, 8, FR, GW), F32),
        V((NG, 8, FR, GW), F32),
        V((NG, 8, FR, GW), BF16),
        V((NG, 3, 2, FR, GW), BF16),
        V((NG, 2, FR, GW), F32),
        V((NG, FR, GW), F32),
        V((NG, 104, GW), F32),
        V((NG, 16, 8, GW), F32),
        V((NG, 7, 2, 8, GW), F32),
        V((NG, 2, 8, GW), F32),
        V((NG, 8, GW), F32),
    ]
    hbm = pl.BlockSpec(memory_space=pl.ANY)
    vmem = pl.BlockSpec(memory_space=pltpu.VMEM)
    smem = pl.BlockSpec(memory_space=pltpu.SMEM)
    return pl.pallas_call(
        kernel,
        out_shape=(
            jax.ShapeDtypeStruct((ROWS, D), BF16),
            jax.ShapeDtypeStruct((ROWS, D), BF16),
            jax.ShapeDtypeStruct((6, D), F32),
            jax.ShapeDtypeStruct((ROWS, D), F32),
            jax.ShapeDtypeStruct((ROWS, D), F32),
        ),
        in_specs=[smem, smem, hbm, hbm, hbm, hbm, vmem],
        out_specs=(vmem,) * 5,
        scratch_shapes=scratch,
        compiler_params=pltpu.CompilerParams(
            collective_id=0, has_side_effects=True, vmem_limit_bytes=60 << 20
        ),
        cost_estimate=pl.CostEstimate(flops=4_000_000_000, bytes_accessed=8_000_000, transcendentals=1_200_000),
        name="joint",
    )(win_start, win_count, video, audio_keys, audio_values, d_out, query_weight)


def solution(mesh):
    spec = P(("frame", "head"), None)
    vec = P(("frame", "head"))
    return jax.shard_map(
        shards,
        mesh=mesh,
        in_specs=(spec, spec, spec, spec, spec, vec, vec),
        out_specs=(spec,) * 5,
        check_vma=False,
    )
```

time: 1120 us -> 114 us (0.10)
  waiting for transfers between devices: 944 us -> 0 us
  Pallas kernels: 0 us -> 106 us
  matrix products: 71.8 us -> 0 us
  local copies, waits for them, and re-layouts: 51.2 us -> 5.58 us
  starting transfers between devices: 30.6 us -> 0 us
  between operations: 15.7 us -> 1.95 us
    all_gather x1 -> x0, waiting for transfers between devices: 672 us -> none  [shards(): lax.all_gather(query_weight, ('frame', 'head'), axis=0, tiled=True)]
    unnamed x3 -> x0, waiting for transfers between devices: 219 us -> none
    pallas_call x0 -> x1, Pallas kernels: none -> 106 us  [shards(): pl.pallas_call(kernel, out_shape=(jax.ShapeDtypeStruct((ROWS, D), BF16),...]
    dot_general x18 -> x0, matrix products: 64.5 us -> none  [the longest x3 17.9 us: attend(): jnp.einsum('hrl,rhd->lhd', score_grad, query_heads, preferred_element_typ...]
    ppermute x8 -> x0, waiting for transfers between devices: 52.3 us -> none  [from_behind(): return lax.ppermute(block, axis, route)]
    ppermute x8 -> x0, starting transfers between devices: 30.5 us -> none  [from_behind(): return lax.ppermute(block, axis, route)]
    unnamed x63 -> x13, local copies, waits for them, and re-layouts: 26.2 us -> 5.58 us
    reshape x12 -> x0, local copies, waits for them, and re-layouts: 17.8 us -> none  [the longest x3 7.42 us: attend(): value_grad.reshape(length, head_count * HEAD_DIM)]
  transfers between devices with their start and end apart: 10 -> 0, of which waited for: 7 -> 0; matrix products, arithmetic and copies ran while one was open for 6% -> 0% of each run, Pallas kernels for 0% -> 0%
where the time goes in v1:
time: 114 us; the launch traced here: 113 us
  Pallas kernels  106 us (93%)
  local copies, waits for them, and re-layouts  5.58 us (5%)
  between operations  1.95 us (2%)
    pallas_call x1, Pallas kernels, shards(): pl.pallas_call(kernel, out_shape=(jax.ShapeDtypeStruct((ROWS, D), BF16),...  106 us
    unnamed x13, local copies, waits for them, and re-layouts  5.58 us

profile of v1, /device:TPU:32, one launch (start us, length us, event | category | flops | bytes accessed | tf_op | source)
XLA Modules:
  0.0 113.2 jit_solution(13907747229327489386)
XLA Ops:
  1.9 105.7 %joint.1 = (bf16[128,1536]{1,0:T(8,128)(2,1)}, bf16[128,1536]{1,0:T(8,128)(2,1)}, f32[6,1536]{1,0:T(8,128)}, f32[128,1536]{1,0:T(8,128)}, f32[128,1536]{1,0:T(8,128)}) custom-call(s32[1]{0:T(128)S(6)} %copy.17.ws_ref, s32[1]{0:T(128)S(6)} %copy.18.wc_ref, bf16[128,1536]{1,0:T(8,128)(2,1)} %video.1, bf16[128,1536]{1,0:T(8,128)(2,1)} %keys.1, ...), custom_call_target="tpu_custom_call" | custom-call | flops 4000000000 | bytes 8000000 | tf_op jit(solution)/shard_map/joint/pallas_call | solution.py:418
  107.6 0.0 copy-start.2
  107.6 0.0 copy-start.1
  107.7 1.9 %copy.19 = bf16[128,1536]{1,0:T(8,128)(2,1)} copy(bf16[128,1536]{1,0:T(8,128)(2,1)} %get-tuple-element.10) | data formatting | bytes 786432
  109.5 0.0 copy-done.2
  109.5 0.0 copy-start.3
  109.5 0.7 copy.20
  110.3 0.1 copy-done.3
  110.3 0.6 copy.21
  110.9 0.0 copy-done.1
  110.9 0.0 copy-start
  110.9 0.9 copy.22
  111.8 0.5 copy-done
  112.4 0.9 copy.23
Async XLA Ops:
  107.6 1.9 %copy-start.2 = (bf16[128,1536]{1,0:T(8,128)(2,1)S(1)}, bf16[128,1536]{1,0:T(8,128)(2,1)}, u32[]{:S(2)}) copy-start(bf16[128,1536]{1,0:T(8,128)(2,1)} %get-tuple-element.11) | copy-start | bytes 1179652
  107.6 3.3 %copy-start.1 = (f32[128,1536]{1,0:T(8,128)S(1)}, f32[128,1536]{1,0:T(8,128)}, u32[]{:S(2)}) copy-start(f32[128,1536]{1,0:T(8,128)} %get-tuple-element.13) | copy-start | bytes 2359300
  109.5 0.8 copy-start.3
  110.9 1.4 %copy-start = (f32[128,1536]{1,0:T(8,128)S(1)}, f32[128,1536]{1,0:T(8,128)}, u32[]{:S(2)}) copy-start(f32[128,1536]{1,0:T(8,128)} %get-tuple-element.14) | copy-start | bytes 2359300

commit v2 on v1

v2 whole, which is shorter than its diff:
```python
import math

import jax
import jax.numpy as jnp
from jax import lax
from jax.experimental import pallas as pl
from jax.experimental.pallas import tpu as pltpu
from jax.sharding import PartitionSpec as P

MESH = pl.DeviceIdType.MESH
HD = 128
D = 1536
HALF = 768
ROWS = 128
NG = 3
GW = HALF // NG
FR = 96
SCALE = 1.0 / math.sqrt(HD)
F32 = jnp.float32
BF16 = jnp.bfloat16
NSEM = 160


def dot(a, b, ca, cb):
    return lax.dot_general(a, b, (((ca,), (cb,)), ((), ())), preferred_element_type=F32)


def kernel(
    ws_ref, wc_ref, video, keys, values, d_out, w_ref,
    att_out, gvid_out, wg_out, gk_out, gv_out,
    ssem, rsem, lsem,
    win, wf, w_send, w4, w_pack, wz, w_tmp, w_full,
    vid, vid_t, k_buf, v_buf, do_buf, q_buf, mask, att_buf, qg_buf,
    gh_send, gh_recv, g_mid, x_send, x_recv, gv_send, gv_recv, gv_own,
    wgp, e_recv, d_send, d_recv, b_tmp, b_part, b_send, b_recv, a_tmp, a_part, a_recv,
):
    f = lax.axis_index("frame")
    h = lax.axis_index("head")
    s = lax.rem(h, 2)
    z = h // 2
    x_lo = f // 8
    y = lax.rem(f // 2, 4)
    core = lax.rem(f, 2)
    p = f * 16 + h

    partner = (f, z * 2 + 1 - s)

    def z_dev(d):
        return (f, lax.rem(z + d, 8) * 2 + s)

    def y_of(d):
        return lax.rem(y + d, 4)

    def y_dev(d):
        return (x_lo * 8 + y_of(d) * 2 + core, h)

    xlo_dev = ((1 - x_lo) * 8 + y * 2 + core, h)
    diag_dev = ((1 - x_lo) * 8 + y * 2 + core, z * 2 + 1 - s)
    core_dev = (x_lo * 8 + y * 2 + 1 - core, h)

    def halo_dev(d):
        q = lax.rem(p + d + 256, 256)
        return (q // 16, lax.rem(q, 16))

    def mine(g):
        return pl.ds(pl.multiple_of(s * HALF + g * GW, 128), GW)

    def theirs(g):
        return pl.ds(pl.multiple_of((1 - s) * HALF + g * GW, 128), GW)

    count = [0]
    sent = []

    def remote(src, dst, dev):
        i = count[0]
        count[0] += 1
        cp = pltpu.make_async_remote_copy(
            src_ref=src, dst_ref=dst, send_sem=ssem.at[i], recv_sem=rsem.at[i],
            device_id=dev, device_id_type=MESH,
        )
        sent.append(cp)
        return cp

    local = [
        pltpu.make_async_copy(video, vid.at[0:ROWS], lsem.at[0]),
        pltpu.make_async_copy(keys.at[:, pl.ds(pl.multiple_of(s * HALF, 128), HALF)], k_buf.at[256:384], lsem.at[1]),
        pltpu.make_async_copy(values.at[:, pl.ds(pl.multiple_of(s * HALF, 128), HALF)], v_buf.at[256:384], lsem.at[2]),
        pltpu.make_async_copy(d_out.at[:, pl.ds(pl.multiple_of(s * HALF, 128), HALF)], do_buf.at[0:ROWS], lsem.at[3]),
    ]
    for cp in local:
        cp.start()

    barrier = pltpu.get_barrier_semaphore()
    peers = [partner] + [z_dev(d) for d in range(1, 8)] + [y_dev(d) for d in range(1, 4)]
    peers += [xlo_dev, diag_dev, core_dev, halo_dev(-2), halo_dev(2)]
    for dev in peers:
        pl.semaphore_signal(barrier, inc=1, device_id=dev, device_id_type=MESH)

    win[0, 0] = jnp.full((8, 128), ws_ref[0], jnp.int32)
    win[0, 1] = jnp.full((8, 128), ws_ref[0] + wc_ref[0], jnp.int32)
    wf[...] = jnp.zeros_like(wf)
    wf[0:6, :] = w_ref[...].astype(F32)
    for k in range(2):
        for ct in range(0, 6, 2):
            col = k * HALF + ct * 128
            pair = jnp.concatenate([wf[:, col : col + 128], wf[:, col + 128 : col + 256]], axis=0)
            w_send[k, ct * 8 : ct * 8 + 16, :] = pair.astype(BF16)

    pl.semaphore_wait(barrier, len(peers))

    here = x_lo * 2 + s
    wa = [
        remote(w_send.at[1 - s], w4.at[here], partner),
        remote(w_send.at[s], w4.at[here], xlo_dev),
        remote(w_send.at[1 - s], w4.at[here], diag_dev),
    ]
    for cp in wa:
        cp.start()
    wl = pltpu.make_async_copy(w_send.at[s], w4.at[here], lsem.at[4])
    wl.start()
    win_cp = remote(win.at[0], win.at[1], partner)
    win_cp.start()
    kx, vx, dx = [], [], []
    for g in range(NG):
        c = pl.ds(g * GW, GW)
        kx.append(remote(keys.at[:, theirs(g)], k_buf.at[384:512, c], partner))
        vx.append(remote(values.at[:, theirs(g)], v_buf.at[384:512, c], partner))
        dx.append(remote(d_out.at[:, theirs(g)], do_buf.at[ROWS : 2 * ROWS, c], partner))
    vid_cp = remote(video, vid.at[ROWS : 2 * ROWS], partner)
    for cp in (kx[0], vx[0], kx[1], vx[1], vid_cp, dx[0], kx[2], vx[2], dx[1], dx[2]):
        cp.start()

    halo_own = []
    for g in range(NG):
        c = pl.ds(g * GW, GW)
        for d in (-2, 2):
            at = 0 if d == 2 else 512
            halo_own.append(remote(keys.at[:, mine(g)], k_buf.at[at : at + 128, c], halo_dev(d)))
            halo_own.append(remote(values.at[:, mine(g)], v_buf.at[at : at + 128, c], halo_dev(d)))
    for cp in halo_own[0:4]:
        cp.start()

    wl.wait()
    for cp in wa:
        cp.wait_recv()
    parts = [w4[i].astype(F32) for i in range(4)]
    for ct in range(6):
        for i in range(4):
            w_pack[ct * 24 + i * 6 : ct * 24 + i * 6 + 8, :] = parts[i][ct * 8 : ct * 8 + 8, :]
    wz[z] = w_pack[0:144, :].astype(BF16)
    zb = []
    for d in range(1, 8):
        zb.append(remote(wz.at[z], wz.at[z], z_dev(d)))
        zb[-1].start()
    for cp in halo_own[4:]:
        cp.start()

    for cp in zb:
        cp.wait_recv()
    for i in range(8):
        w_pack[0:144, :] = wz[i].astype(F32)
        for ct in range(6):
            for xl in range(2):
                w_tmp[xl, 12 * i : 12 * i + 16, ct * 128 : ct * 128 + 128] = w_pack[ct * 24 + xl * 12 : ct * 24 + xl * 12 + 16, :]
    own = y * 2 + core
    for xl in range(2):
        w_full[xl, own] = w_tmp[xl, 0:FR, :].astype(BF16)

    dy, e_cps = [], []
    for g in range(NG):
        c = pl.ds(g * GW, GW)
        part = w_full.at[:, own, :, c]
        dy.append([remote(part, part, y_dev(d)) for d in range(1, 4)])
        e_cps.append([remote(part, part, core_dev)])
        for cp in dy[g] + e_cps[g]:
            cp.start()

    halo_par = []

    def pass_on(g):
        c = pl.ds(g * GW, GW)
        kx[g].wait_recv()
        vx[g].wait_recv()
        for d in (-2, 2):
            at = 128 if d == 2 else 640
            for buf in (k_buf, v_buf):
                halo_par.append(remote(buf.at[384:512, c], buf.at[at : at + 128, c], halo_dev(d)))
                halo_par[-1].start()

    def to_core(g):
        c = pl.ds(g * GW, GW)
        for d in range(1, 4):
            dy[g][d - 1].wait_recv()
            part = w_full.at[:, lax.rem(y + 4 - d, 4) * 2 + core, :, c]
            e_cps[g].append(remote(part, part, core_dev))
            e_cps[g][-1].start()

    pass_on(0)
    pass_on(1)

    win_cp.wait_recv()
    for half in range(2):
        lo = win[half, 0, 0:1, :]
        hi = win[half, 1, 0:1, :]
        for j in range(6):
            base = p if j % 2 == 0 else p + 1 - 2 * s
            blk = base + 2 * (j // 2 - 1)
            ok = jnp.logical_and(lo <= blk, blk < hi)
            bias = jnp.where(ok, 0.0, -1e30).astype(F32)
            mask[half * 128 : half * 128 + 128, j * 128 : j * 128 + 128] = jnp.broadcast_to(bias, (128, 128))

    to_core(0)

    for cp in local:
        cp.wait()
    vid_cp.wait_recv()
    for i in range(0, D, 256):
        vid_t[i : i + 256, :] = vid[:, i : i + 256].T

    att_cps, gh_cps, xr_cps = [], [], []

    def project(g):
        c0 = g * GW
        for cp in e_cps[g]:
            cp.wait_recv()
        w = w_full[:, :, :, c0 : c0 + GW].reshape(D, GW)
        q_buf[:, c0 : c0 + GW] = dot(vid[...], w, 1, 0).astype(BF16)
        for cp in halo_own[4 * g : 4 * g + 4] + halo_par[4 * g : 4 * g + 4]:
            cp.wait_recv()
        dx[g].wait_recv()

    def head(g, hh):
        c = pl.ds(g * GW + hh * HD, HD)
        q = q_buf[:, c]
        k = k_buf[:, c]
        v = v_buf[:, c]
        do = do_buf[:, c]
        sc = dot(q, k, 1, 1) * SCALE + mask[...]
        top = jnp.max(sc, axis=-1, keepdims=True)
        e = jnp.exp(sc - top)
        prob = e * (1.0 / jnp.sum(e, axis=-1, keepdims=True))
        half = prob.astype(BF16)
        att_buf[:, c] = dot(half, v, 1, 0).astype(BF16)
        pg = dot(do, v, 1, 1)
        delta = jnp.sum(prob * pg, axis=-1, keepdims=True)
        ds = (prob * (pg - delta) * SCALE).astype(BF16)
        qg_buf[:, c] = dot(ds, k, 1, 0).astype(BF16)
        gk = dot(ds, q, 0, 0)
        gv = dot(half, do, 0, 0)
        for i, gr in enumerate((gk, gv)):
            gh_send[0, i, :, c] = gr[0:256].astype(BF16)
            g_mid[i, :, c] = gr[256:512]
            gh_send[1, i, :, c] = gr[512:768].astype(BF16)
        for i, d in enumerate((-2, 2)):
            gh_cps.append(remote(gh_send.at[i, :, :, c], gh_recv.at[i, :, :, c], halo_dev(d)))
            gh_cps[-1].start()

    def send_group(g):
        c0 = g * GW
        c = pl.ds(c0, GW)
        att_cps.append(remote(att_buf.at[ROWS : 2 * ROWS, c], att_out.at[:, mine(g)], partner))
        att_cps[-1].start()
        att_out[:, mine(g)] = att_buf[0:ROWS, c0 : c0 + GW]

    ecs, dcs, bcs, acs = [], [], [], []

    def weight_term(g):
        c0 = g * GW
        for i in range(0, 16, 4):
            r = dot(vid_t[i * FR : (i + 4) * FR, :], qg_buf[:, c0 : c0 + GW], 1, 0)
            for j in range(4):
                fr = i + j
                wgp[g, fr % 2, (fr // 2 % 4) * 2 + fr // 8] = r[j * FR : (j + 1) * FR]
        ecs.append(remote(wgp.at[g, 1 - core], e_recv.at[g], core_dev))
        ecs[g].start()

    def halo_back(k):
        c0 = k * HD
        for cp in gh_cps[2 * k : 2 * k + 2]:
            cp.wait_recv()
        for i, out in enumerate((gk_out, gv_out)):
            tot = g_mid[i, :, c0 : c0 + HD]
            tot = tot + gh_recv[0, i, :, c0 : c0 + HD].astype(F32) + gh_recv[1, i, :, c0 : c0 + HD].astype(F32)
            out[:, pl.ds(pl.multiple_of(s * HALF + c0, 128), HD)] = tot[0:ROWS]
            x_send[i, :, c0 : c0 + HD] = tot[ROWS:].astype(BF16)
        c = pl.ds(c0, HD)
        xr_cps.append(remote(x_send.at[:, :, c], x_recv.at[:, :, c], partner))
        xr_cps[-1].start()

    def stage_d(g):
        ecs[g].wait_recv()
        for i in range(8):
            d_send[g, i] = (wgp[g, core, i] + e_recv[g, i]).astype(BF16)
        cps = []
        for d in range(1, 4):
            cps.append(remote(d_send.at[g, pl.ds(y_of(d) * 2, 2)], d_recv.at[g, d - 1], y_dev(d)))
            cps[-1].start()
        dcs.append(cps)

    def stage_b(g):
        for cp in dcs[g]:
            cp.wait_recv()
        for xl in range(2):
            t = wgp[g, core, y * 2 + xl] + e_recv[g, y * 2 + xl]
            for d in range(3):
                t = t + d_recv[g, d, xl].astype(F32)
            b_tmp[g, xl, 0:FR, :] = t
        for i in range(8):
            for ct in range(2):
                for xl in range(2):
                    at = ct * 24 + xl * 12
                    b_part[g, i, at : at + 16, :] = b_tmp[g, xl, 12 * i : 12 * i + 16, ct * 128 : ct * 128 + 128]
            b_send[g, i] = b_part[g, i, 0:48].astype(BF16)
        cps = []
        for d in range(1, 8):
            cps.append(remote(b_send.at[g, lax.rem(z + d, 8)], b_recv.at[g, d - 1], z_dev(d)))
            cps[-1].start()
        bcs.append(cps)

    def stage_a(g):
        for cp in bcs[g]:
            cp.wait_recv()
        t = b_part[g, z, 0:48]
        for d in range(7):
            t = t + b_recv[g, d].astype(F32)
        a_tmp[g, 0:48] = t
        for i in range(4):
            for ct in range(2):
                at = ct * 24 + i * 6
                a_part[g, i, :, ct * 128 : ct * 128 + 128] = a_tmp[g, at : at + 8, :]
        cps = []
        for i, (dev, shard) in enumerate((
            (partner, x_lo * 2 + 1 - s), (xlo_dev, (1 - x_lo) * 2 + s), (diag_dev, (1 - x_lo) * 2 + 1 - s),
        )):
            cps.append(remote(a_part.at[g, shard], a_recv.at[g, i], dev))
            cps[-1].start()
        acs.append(cps)

    b_tmp[...] = jnp.zeros_like(b_tmp)
    a_tmp[...] = jnp.zeros_like(a_tmp)
    project(0)
    head(0, 0)
    pass_on(2)
    to_core(1)
    head(0, 1)
    send_group(0)
    weight_term(0)
    project(1)
    head(1, 0)
    to_core(2)
    stage_d(0)
    head(1, 1)
    send_group(1)
    weight_term(1)
    halo_back(0)
    project(2)
    head(2, 0)
    stage_d(1)
    halo_back(1)
    head(2, 1)
    send_group(2)
    weight_term(2)
    stage_b(0)
    def w_rows(i):
        return w_full[i // 768, i // 96 % 8 : i // 96 % 8 + 4].reshape(384, HALF)

    gvc = []
    for i in range(0, D, 384):
        gv_send[:, i : i + 384] = dot(qg_buf[ROWS:, :], w_rows(i), 1, 1).astype(BF16)
        gvc.append(remote(gv_send.at[:, i : i + 384], gv_recv.at[:, i : i + 384], partner))
        gvc[-1].start()
    halo_back(2)
    stage_d(2)
    halo_back(3)
    stage_b(1)
    for i in range(0, D, 384):
        gv_own[:, i : i + 384] = dot(qg_buf[0:ROWS, :], w_rows(i), 1, 1)
    stage_a(0)
    halo_back(4)
    halo_back(5)
    stage_b(2)
    stage_a(1)
    stage_a(2)

    for g in range(NG):
        xr_cps[2 * g].wait_recv()
        xr_cps[2 * g + 1].wait_recv()
        c0 = g * GW
        for i, out in enumerate((gk_out, gv_out)):
            out[:, theirs(g)] = x_recv[i, :, c0 : c0 + GW].astype(F32)
    for cp in gvc:
        cp.wait_recv()
    gvid_out[...] = (gv_own[...] + gv_recv[...].astype(F32)).astype(BF16)
    for g in range(NG):
        for cp in acs[g]:
            cp.wait_recv()
        wg_out[:, mine(g)] = (a_part[g, here] + a_recv[g, 1])[0:6]
        wg_out[:, theirs(g)] = (a_recv[g, 0] + a_recv[g, 2])[0:6]
        att_cps[g].wait_recv()
    for cp in sent:
        cp.wait_send()
    assert count[0] <= NSEM


def shards(video, audio_keys, audio_values, query_weight, d_out, win_start, win_count):
    V = pltpu.VMEM
    sem = pltpu.SemaphoreType.DMA
    scratch = [
        sem((NSEM,)), sem((NSEM,)), sem((8,)),
        V((2, 2, 8, 128), jnp.int32),
        V((8, D), F32),
        V((2, 48, 128), BF16),
        V((4, 48, 128), BF16),
        V((152, 128), F32),
        V((8, 144, 128), BF16),
        V((2, 104, HALF), F32),
        V((2, 8, FR, HALF), BF16),
        V((256, D), BF16),
        V((D, 256), BF16),
        V((768, HALF), BF16),
        V((768, HALF), BF16),
        V((256, HALF), BF16),
        V((256, HALF), BF16),
        V((256, 768), F32),
        V((256, HALF), BF16),
        V((256, HALF), BF16),
        V((2, 2, 256, HALF), BF16),
        V((2, 2, 256, HALF), BF16),
        V((2, 256, HALF), F32),
        V((2, ROWS, HALF), BF16),
        V((2, ROWS, HALF), BF16),
        V((ROWS, D), BF16),
        V((ROWS, D), BF16),
        V((ROWS, D), F32),
        V((NG, 2, 8, FR, GW), F32),
        V((NG, 8, FR, GW), F32),
        V((NG, 8, FR, GW), BF16),
        V((NG, 3, 2, FR, GW), BF16),
        V((NG, 2, 104, GW), F32),
        V((NG, 8, 56, 128), F32),
        V((NG, 8, 48, 128), BF16),
        V((NG, 7, 48, 128), BF16),
        V((NG, 56, 128), F32),
        V((NG, 4, 8, GW), F32),
        V((NG, 3, 8, GW), F32),
    ]
    hbm = pl.BlockSpec(memory_space=pl.ANY)
    vmem = pl.BlockSpec(memory_space=pltpu.VMEM)
    smem = pl.BlockSpec(memory_space=pltpu.SMEM)
    return pl.pallas_call(
        kernel,
        out_shape=(
            jax.ShapeDtypeStruct((ROWS, D), BF16),
            jax.ShapeDtypeStruct((ROWS, D), BF16),
            jax.ShapeDtypeStruct((6, D), F32),
            jax.ShapeDtypeStruct((ROWS, D), F32),
            jax.ShapeDtypeStruct((ROWS, D), F32),
        ),
        in_specs=[smem, smem, hbm, hbm, hbm, hbm, vmem],
        out_specs=(vmem,) * 5,
        scratch_shapes=scratch,
        compiler_params=pltpu.CompilerParams(
            collective_id=0, has_side_effects=True, vmem_limit_bytes=60 << 20
        ),
        cost_estimate=pl.CostEstimate(flops=4_000_000_000, bytes_accessed=8_000_000, transcendentals=1_200_000),
        name="joint",
    )(win_start, win_count, video, audio_keys, audio_values, d_out, query_weight)


def solution(mesh):
    spec = P(("frame", "head"), None)
    vec = P(("frame", "head"))
    return jax.shard_map(
        shards,
        mesh=mesh,
        in_specs=(spec, spec, spec, spec, spec, vec, vec),
        out_specs=(spec,) * 5,
        check_vma=False,
    )
```

time: 114 us -> 85.1 us (0.75)
  Pallas kernels: 106 us -> 76.2 us
    pallas_call x1, Pallas kernels: 106 us -> 76.2 us  [shards(): pl.pallas_call(kernel, out_shape=(jax.ShapeDtypeStruct((ROWS, D), BF16),...]
where the time goes in v2:
time: 85.1 us; the launch traced here: 83.7 us
  Pallas kernels  76.2 us (90%)
  local copies, waits for them, and re-layouts  5.58 us (7%)
  between operations  1.95 us (2%)
    pallas_call x1, Pallas kernels, shards(): pl.pallas_call(kernel, out_shape=(jax.ShapeDtypeStruct((ROWS, D), BF16),...  76.2 us
    unnamed x13, local copies, waits for them, and re-layouts  5.58 us

profile of v2, /device:TPU:32, one launch (start us, length us, event | category | flops | bytes accessed | tf_op | source)
XLA Modules:
  0.0 83.7 jit_solution(1129608618326409517)
XLA Ops:
  1.9 76.2 %joint.1 = (bf16[128,1536]{1,0:T(8,128)(2,1)}, bf16[128,1536]{1,0:T(8,128)(2,1)}, f32[6,1536]{1,0:T(8,128)}, f32[128,1536]{1,0:T(8,128)}, f32[128,1536]{1,0:T(8,128)}) custom-call(s32[1]{0:T(128)S(6)} %copy.17.ws_ref, s32[1]{0:T(128)S(6)} %copy.18.wc_ref, bf16[128,1536]{1,0:T(8,128)(2,1)} %video.1, bf16[128,1536]{1,0:T(8,128)(2,1)} %keys.1, ...), custom_call_target="tpu_custom_call" | custom-call | flops 4000000000 | bytes 8000000 | tf_op jit(solution)/shard_map/joint/pallas_call | solution.py:450
  78.1 0.0 copy-start.2
  78.1 0.0 copy-start.1
  78.1 1.9 %copy.19 = bf16[128,1536]{1,0:T(8,128)(2,1)} copy(bf16[128,1536]{1,0:T(8,128)(2,1)} %get-tuple-element.10) | data formatting | bytes 786432
  80.0 0.0 copy-done.2
  80.0 0.0 copy-start.3
  80.0 0.7 copy.20
  80.7 0.1 copy-done.3
  80.8 0.6 copy.21
  81.4 0.0 copy-done.1
  81.4 0.0 copy-start
  81.4 0.9 %copy.22 = f32[128,1536]{1,0:T(8,128)} copy(f32[128,1536]{1,0:T(8,128)S(1)} %copy-done.1) | data formatting | bytes 1572864
  82.3 0.5 copy-done
  82.8 0.9 %copy.23 = f32[128,1536]{1,0:T(8,128)} copy(f32[128,1536]{1,0:T(8,128)S(1)} %copy-done) | data formatting | bytes 1572864
Async XLA Ops:
  78.1 1.9 %copy-start.2 = (bf16[128,1536]{1,0:T(8,128)(2,1)S(1)}, bf16[128,1536]{1,0:T(8,128)(2,1)}, u32[]{:S(2)}) copy-start(bf16[128,1536]{1,0:T(8,128)(2,1)} %get-tuple-element.11) | copy-start | bytes 1179652
  78.1 3.3 %copy-start.1 = (f32[128,1536]{1,0:T(8,128)S(1)}, f32[128,1536]{1,0:T(8,128)}, u32[]{:S(2)}) copy-start(f32[128,1536]{1,0:T(8,128)} %get-tuple-element.13) | copy-start | bytes 2359300
  80.0 0.8 copy-start.3
  81.4 1.4 %copy-start = (f32[128,1536]{1,0:T(8,128)S(1)}, f32[128,1536]{1,0:T(8,128)}, u32[]{:S(2)}) copy-start(f32[128,1536]{1,0:T(8,128)} %get-tuple-element.14) | copy-start | bytes 2359300

commit v3 on v2

--- a/solution.py
+++ b/solution.py
@@ -21,6 +21,15 @@
 NSEM = 160
 
 
+OUTS = (
+    ((ROWS, D), BF16),
+    ((ROWS, D), BF16),
+    ((6, D), F32),
+    ((ROWS, D), F32),
+    ((ROWS, D), F32),
+)
+
+
 def dot(a, b, ca, cb):
     return lax.dot_general(a, b, (((ca,), (cb,)), ((), ())), preferred_element_type=F32)
 
@@ -30,7 +39,7 @@
     att_out, gvid_out, wg_out, gk_out, gv_out,
     ssem, rsem, lsem,
     win, wf, w_send, w4, w_pack, wz, w_tmp, w_full,
-    vid, vid_t, k_buf, v_buf, do_buf, q_buf, mask, att_buf, qg_buf,
+    vid, vid_t, kv, do_buf, q_buf, mask, att_buf, qg_buf,
     gh_send, gh_recv, g_mid, x_send, x_recv, gv_send, gv_recv, gv_own,
     wgp, e_recv, d_send, d_recv, b_tmp, b_part, b_send, b_recv, a_tmp, a_part, a_recv,
 ):
@@ -83,8 +92,8 @@
 
     local = [
         pltpu.make_async_copy(video, vid.at[0:ROWS], lsem.at[0]),
-        pltpu.make_async_copy(keys.at[:, pl.ds(pl.multiple_of(s * HALF, 128), HALF)], k_buf.at[256:384], lsem.at[1]),
-        pltpu.make_async_copy(values.at[:, pl.ds(pl.multiple_of(s * HALF, 128), HALF)], v_buf.at[256:384], lsem.at[2]),
+        pltpu.make_async_copy(keys.at[:, pl.ds(pl.multiple_of(s * HALF, 128), HALF)], kv.at[0, 256:384], lsem.at[1]),
+        pltpu.make_async_copy(values.at[:, pl.ds(pl.multiple_of(s * HALF, 128), HALF)], kv.at[1, 256:384], lsem.at[2]),
         pltpu.make_async_copy(d_out.at[:, pl.ds(pl.multiple_of(s * HALF, 128), HALF)], do_buf.at[0:ROWS], lsem.at[3]),
     ]
     for cp in local:
@@ -123,22 +132,30 @@
     kx, vx, dx = [], [], []
     for g in range(NG):
         c = pl.ds(g * GW, GW)
-        kx.append(remote(keys.at[:, theirs(g)], k_buf.at[384:512, c], partner))
-        vx.append(remote(values.at[:, theirs(g)], v_buf.at[384:512, c], partner))
+        kx.append(remote(keys.at[:, theirs(g)], kv.at[0, 384:512, c], partner))
+        vx.append(remote(values.at[:, theirs(g)], kv.at[1, 384:512, c], partner))
         dx.append(remote(d_out.at[:, theirs(g)], do_buf.at[ROWS : 2 * ROWS, c], partner))
     vid_cp = remote(video, vid.at[ROWS : 2 * ROWS], partner)
     for cp in (kx[0], vx[0], kx[1], vx[1], vid_cp, dx[0], kx[2], vx[2], dx[1], dx[2]):
         cp.start()
 
-    halo_own = []
-    for g in range(NG):
-        c = pl.ds(g * GW, GW)
+    halo = [[] for _ in range(NG)]
+
+    def halo_send(g, at):
         for d in (-2, 2):
-            at = 0 if d == 2 else 512
-            halo_own.append(remote(keys.at[:, mine(g)], k_buf.at[at : at + 128, c], halo_dev(d)))
-            halo_own.append(remote(values.at[:, mine(g)], v_buf.at[at : at + 128, c], halo_dev(d)))
-    for cp in halo_own[0:4]:
-        cp.start()
+            to = at - 256 if d == 2 else at + 256
+            c = pl.ds(g * GW, GW)
+            halo[g].append(remote(kv.at[:, at : at + 128, c], kv.at[:, to : to + 128, c], halo_dev(d)))
+            halo[g][-1].start()
+
+    def pass_on(g):
+        kx[g].wait_recv()
+        vx[g].wait_recv()
+        halo_send(g, 384)
+
+    for cp in local:
+        cp.wait()
+    halo_send(0, 256)
 
     wl.wait()
     for cp in wa:
@@ -152,8 +169,8 @@
     for d in range(1, 8):
         zb.append(remote(wz.at[z], wz.at[z], z_dev(d)))
         zb[-1].start()
-    for cp in halo_own[4:]:
-        cp.start()
+    pass_on(0)
+    halo_send(1, 256)
 
     for cp in zb:
         cp.wait_recv()
@@ -175,18 +192,6 @@
         for cp in dy[g] + e_cps[g]:
             cp.start()
 
-    halo_par = []
-
-    def pass_on(g):
-        c = pl.ds(g * GW, GW)
-        kx[g].wait_recv()
-        vx[g].wait_recv()
-        for d in (-2, 2):
-            at = 128 if d == 2 else 640
-            for buf in (k_buf, v_buf):
-                halo_par.append(remote(buf.at[384:512, c], buf.at[at : at + 128, c], halo_dev(d)))
-                halo_par[-1].start()
-
     def to_core(g):
         c = pl.ds(g * GW, GW)
         for d in range(1, 4):
@@ -195,8 +200,8 @@
             e_cps[g].append(remote(part, part, core_dev))
             e_cps[g][-1].start()
 
-    pass_on(0)
     pass_on(1)
+    halo_send(2, 256)
 
     win_cp.wait_recv()
     for half in range(2):
@@ -211,8 +216,6 @@
 
     to_core(0)
 
-    for cp in local:
-        cp.wait()
     vid_cp.wait_recv()
     for i in range(0, D, 256):
         vid_t[i : i + 256, :] = vid[:, i : i + 256].T
@@ -225,15 +228,15 @@
             cp.wait_recv()
         w = w_full[:, :, :, c0 : c0 + GW].reshape(D, GW)
         q_buf[:, c0 : c0 + GW] = dot(vid[...], w, 1, 0).astype(BF16)
-        for cp in halo_own[4 * g : 4 * g + 4] + halo_par[4 * g : 4 * g + 4]:
+        for cp in halo[g]:
             cp.wait_recv()
         dx[g].wait_recv()
 
     def head(g, hh):
         c = pl.ds(g * GW + hh * HD, HD)
         q = q_buf[:, c]
-        k = k_buf[:, c]
-        v = v_buf[:, c]
+        k = kv[0, :, c]
+        v = kv[1, :, c]
         do = do_buf[:, c]
         sc = dot(q, k, 1, 1) * SCALE + mask[...]
         top = jnp.max(sc, axis=-1, keepdims=True)
@@ -340,14 +343,14 @@
     a_tmp[...] = jnp.zeros_like(a_tmp)
     project(0)
     head(0, 0)
-    pass_on(2)
     to_core(1)
     head(0, 1)
+    pass_on(2)
     send_group(0)
     weight_term(0)
+    to_core(2)
     project(1)
     head(1, 0)
-    to_core(2)
     stage_d(0)
     head(1, 1)
     send_group(1)
@@ -417,8 +420,7 @@
         V((2, 8, FR, HALF), BF16),
         V((256, D), BF16),
         V((D, 256), BF16),
-        V((768, HALF), BF16),
-        V((768, HALF), BF16),
+        V((2, 768, HALF), BF16),
         V((256, HALF), BF16),
         V((256, HALF), BF16),
         V((256, 768), F32),
@@ -447,15 +449,9 @@
     hbm = pl.BlockSpec(memory_space=pl.ANY)
     vmem = pl.BlockSpec(memory_space=pltpu.VMEM)
     smem = pl.BlockSpec(memory_space=pltpu.SMEM)
-    return pl.pallas_call(
+    outs = pl.pallas_call(
         kernel,
-        out_shape=(
-            jax.ShapeDtypeStruct((ROWS, D), BF16),
-            jax.ShapeDtypeStruct((ROWS, D), BF16),
-            jax.ShapeDtypeStruct((6, D), F32),
-            jax.ShapeDtypeStruct((ROWS, D), F32),
-            jax.ShapeDtypeStruct((ROWS, D), F32),
-        ),
+        out_shape=tuple(V(shape, kind) for shape, kind in OUTS),
         in_specs=[smem, smem, hbm, hbm, hbm, hbm, vmem],
         out_specs=(vmem,) * 5,
         scratch_shapes=scratch,
@@ -465,6 +461,7 @@
         cost_estimate=pl.CostEstimate(flops=4_000_000_000, bytes_accessed=8_000_000, transcendentals=1_200_000),
         name="joint",
     )(win_start, win_count, video, audio_keys, audio_values, d_out, query_weight)
+    return outs
 
 
 def solution(mesh):

time: 85.1 us -> 82.9 us (0.974)
  the two profiles are of different devices: /device:TPU:32 before, /device:TPU:25 now
where the time goes in v3:
time: 82.9 us; the launch traced here: 82.7 us
  Pallas kernels  76.9 us (93%)
  local copies, waits for them, and re-layouts  3.87 us (5%)
  between operations  1.93 us (2%)
    pallas_call x1, Pallas kernels, shards(): pl.pallas_call(kernel, out_shape=tuple((V(shape, kind) for shape, kind in...  76.9 us
    unnamed x5, local copies, waits for them, and re-layouts  3.87 us

profile of v3, /device:TPU:25, one launch (start us, length us, event | category | flops | bytes accessed | tf_op | source)
XLA Modules:
  0.0 82.7 jit_solution(10498516248099127350)
XLA Ops:
  1.9 76.9 %joint.1 = (bf16[128,1536]{1,0:T(8,128)(2,1)S(1)}, bf16[128,1536]{1,0:T(8,128)(2,1)S(1)}, f32[6,1536]{1,0:T(8,128)S(1)}, f32[128,1536]{1,0:T(8,128)S(1)}, f32[128,1536]{1,0:T(8,128)S(1)}) custom-call(s32[1]{0:T(128)S(6)} %copy.22.ws_ref, s32[1]{0:T(128)S(6)} %copy.23.wc_ref, bf16[128,1536]{1,0:T(8,128)(2,1)} %video.1, bf16[128,1536]{1,0:T(8,128)(2,1)} %keys.1, ...), custom_call_target="tpu_custom_call" | custom-call | flops 4000000000 | bytes 8000000 | tf_op jit(solution)/shard_map/joint/pallas_call | solution.py:452
  78.9 0.7 copy.17
  79.6 0.6 copy.19
  80.2 0.7 copy.18
  81.0 0.9 %copy.20 = f32[128,1536]{1,0:T(8,128)} copy(f32[128,1536]{1,0:T(8,128)S(1)} %get-tuple-element.8) | data formatting | bytes 1572864
  81.8 0.9 %copy.21 = f32[128,1536]{1,0:T(8,128)} copy(f32[128,1536]{1,0:T(8,128)S(1)} %get-tuple-element.9) | data formatting | bytes 1572864
